TPU v7x, 256 devices: a whole 4x4x8 slice. The times are simulated.
256 devices in a mesh: row: 16 (over z_hi, x, core), col: 16 (over y, z_lo).
Axes of the slice: x: 4, y: 4, z: 8 (z_hi: 2, z_lo: 4; z = z_hi * 4 + z_lo), core: 2. Of those that a mesh axis runs over, the one named last changes fastest.
Arguments:
- eigvec: float32 [28672, 8192], P('row', 'col'), may hold values from -6 to 6
- householder: float32 [4, 28672, 256], P(None, 'row', 'col'), may hold values from -0.03125 to 0.03125
- panel_factors: float32 [4, 2, 128, 128], replicated, may hold values from -1 to 1.5, as said below
Outputs:
- transformed: float32 [28672, 8192], P('row', 'col')
Inputs may be any that keep to these rules, and one draw needn't show every extreme that they name: Each panel_factors[b, i] is upper triangular.
All inputs are finite; a program needn't handle non-finite values.
Results may differ from a plain program's by a relative error of at most 0.0001.
Values sent between devices are 32-bit elements; how exact they have to be, the bound alone decides.
A program may use at most 64 MiB of HBM per device.

v0:
```python
import jax
import jax.numpy as jnp
from jax import lax
from jax.sharding import PartitionSpec as P


def precise_dot(left, right):
    return jnp.dot(left, right, precision=lax.Precision.HIGHEST, preferred_element_type=jnp.float32)


def rows_product(left, right):
    return lax.dot_general(
        left,
        right,
        (((0,), (0,)), ((), ())),
        precision=lax.Precision.HIGHEST,
        preferred_element_type=jnp.float32,
    )


def apply_block(reflectors, factor, vectors):
    partial_value = rows_product(reflectors, vectors)
    summed = lax.psum(partial_value, "row")
    scaled = precise_dot(factor, summed)
    return vectors - precise_dot(reflectors, scaled)


def per_device(eigvec, householder, panel_factors):
    blocks_here = householder.shape[0]
    panel = panel_factors.shape[2]
    vectors = eigvec
    for window in range(blocks_here):
        reflectors = lax.all_gather(householder[window], "col", axis=1, tiled=True)
        lead_panel = reflectors[:, :panel]
        tail_panel = reflectors[:, panel:]
        lead_factor = panel_factors[window, 0]
        tail_factor = panel_factors[window, 1]
        vectors = apply_block(tail_panel, tail_factor, vectors)
        vectors = apply_block(lead_panel, lead_factor, vectors)
    return vectors


def solution(mesh):
    in_specs = (P("row", "col"), P(None, "row", "col"), P())
    out_specs = P("row", "col")
    return jax.shard_map(
        per_device, mesh=mesh, in_specs=in_specs, out_specs=out_specs, check_vma=False
    )
```

profile of v0, /device:TPU:1, one launch (start us, length us, event | category | flops | bytes accessed | tf_op | source)
XLA Modules:
  0.0 1866.3 jit_solution(8624119980585822286)
XLA Ops:
  6.5 1.8 fusion.41
  8.4 0.0 all-gather.9.cloned.1.call-update
  8.4 0.0 all-reduce.9.cloned.1.call-start
  8.4 81.6 %all-gather.9.cloned.1.call-done = f32[1,1792,256]{1,2,0:T(8,128)} async-done(((f32[1,1792,16]{1,2,0:T(8,128)}), f32[1,1792,256]{1,2,0:T(8,128)}) %all-gather.9.cloned.1.call-update) | async-done | bytes 1835024 | tf_op jit(solution)/shard_map/all_gather | solution.py:33
  90.0 5.2 fusion.15
  95.2 0.0 all-reduce.9.cloned.1.call-update
  95.3 0.0 all-reduce.11.cloned.1.call-start
  95.3 5.3 copy.4
  100.6 178.7 %all-reduce.9.cloned.1.call-done = f32[128,512]{1,0:T(8,128)} async-done(((f32[128,512]{1,0:T(8,128)}), f32[128,512]{1,0:T(8,128)}) %all-reduce.9.cloned.1.call-update) | async-done | bytes 262160 | tf_op jit(solution)/shard_map/psum | solution.py:23
  279.3 1.5 fusion.31
  280.8 5.3 bitcast_subtract_fusion.7
  286.1 1.8 copy-done.1
  288.0 3.7 convolution_bitcast_fusion.6
  291.7 0.0 all-reduce.11.cloned.1.call-update
  291.7 0.0 all-gather.11.cloned.1.call-start
  291.8 0.5 all-gather.11.cloned.1.call-update
  292.3 0.5 all-reduce.13.cloned.1.call-start
  292.8 176.0 %all-reduce.11.cloned.1.call-done = f32[128,512]{0,1:T(8,128)} async-done(((f32[128,512]{0,1:T(8,128)}), f32[128,512]{0,1:T(8,128)}) %all-reduce.11.cloned.1.call-update) | async-done | bytes 262160 | tf_op jit(solution)/shard_map/psum | solution.py:23
  468.8 1.3 fusion.29
  470.2 6.0 bitcast_subtract_fusion.6
  476.1 72.2 %all-gather.11.cloned.1.call-done = f32[1,1792,256]{1,2,0:T(8,128)} async-done(((f32[1,1792,16]{1,2,0:T(8,128)}), f32[1,1792,256]{1,2,0:T(8,128)}) %all-gather.11.cloned.1.call-update) | async-done | bytes 1835024 | tf_op jit(solution)/shard_map/all_gather | solution.py:33
  548.4 6.1 convolution_bitcast_fusion.5
  554.5 0.0 all-reduce.15.cloned.1.call-start
  554.6 184.2 %all-reduce.13.cloned.1.call-done = f32[128,512]{0,1:T(8,128)} async-done(((f32[128,512]{0,1:T(8,128)}), f32[128,512]{0,1:T(8,128)}) %all-reduce.13.cloned.1.call-update) | async-done | bytes 262160 | tf_op jit(solution)/shard_map/psum | solution.py:23
  738.8 1.3 fusion.27
  740.1 5.3 bitcast_subtract_fusion.5
  745.4 1.8 copy-done.2
  747.3 3.7 convolution_bitcast_fusion.4
  751.0 0.0 all-reduce.15.cloned.1.call-update
  751.0 0.0 all-gather.13.cloned.1.call-start
  751.1 0.7 all-gather.13.cloned.1.call-update
  751.8 0.2 all-reduce.17.cloned.1.call-start
  752.0 176.2 %all-reduce.15.cloned.1.call-done = f32[128,512]{0,1:T(8,128)} async-done(((f32[128,512]{0,1:T(8,128)}), f32[128,512]{0,1:T(8,128)}) %all-reduce.15.cloned.1.call-update) | async-done | bytes 262160 | tf_op jit(solution)/shard_map/psum | solution.py:23
  928.2 1.3 fusion.25
  929.6 6.0 bitcast_subtract_fusion.4
  935.5 72.4 %all-gather.13.cloned.1.call-done = f32[1,1792,256]{1,2,0:T(8,128)} async-done(((f32[1,1792,16]{1,2,0:T(8,128)}), f32[1,1792,256]{1,2,0:T(8,128)}) %all-gather.13.cloned.1.call-update) | async-done | bytes 1835024 | tf_op jit(solution)/shard_map/all_gather | solution.py:33
  1007.9 6.1 convolution_bitcast_fusion.3
  1014.1 0.0 all-reduce.19.cloned.1.call-start
  1014.1 184.1 %all-reduce.17.cloned.1.call-done = f32[128,512]{0,1:T(8,128)} async-done(((f32[128,512]{0,1:T(8,128)}), f32[128,512]{0,1:T(8,128)}) %all-reduce.17.cloned.1.call-update) | async-done | bytes 262160 | tf_op jit(solution)/shard_map/psum | solution.py:23
  1198.2 1.3 fusion.23
  1199.5 5.3 bitcast_subtract_fusion.3
  1204.8 1.8 copy-done
  1206.7 3.7 convolution_bitcast_fusion.2
  1210.4 0.0 all-reduce.19.cloned.1.call-update
  1210.4 0.0 all-gather.15.cloned.1.call-start
  1210.5 0.5 all-gather.15.cloned.1.call-update
  1211.0 0.3 all-reduce.21.cloned.1.call-start
  1211.3 176.4 %all-reduce.19.cloned.1.call-done = f32[128,512]{0,1:T(8,128)} async-done(((f32[128,512]{0,1:T(8,128)}), f32[128,512]{0,1:T(8,128)}) %all-reduce.19.cloned.1.call-update) | async-done | bytes 262160 | tf_op jit(solution)/shard_map/psum | solution.py:23
  1387.6 1.3 fusion.21
  1389.0 6.0 bitcast_subtract_fusion.2
  1394.9 72.2 %all-gather.15.cloned.1.call-done = f32[1,1792,256]{1,2,0:T(8,128)} async-done(((f32[1,1792,16]{1,2,0:T(8,128)}), f32[1,1792,256]{1,2,0:T(8,128)}) %all-gather.15.cloned.1.call-update) | async-done | bytes 1835024 | tf_op jit(solution)/shard_map/all_gather | solution.py:33
  1467.2 6.1 convolution_bitcast_fusion.1
  1473.3 0.0 all-reduce.21.cloned.1.call-update
  1473.3 0.0 all-reduce.23.cloned.1.call-start
  1473.4 184.1 %all-reduce.21.cloned.1.call-done = f32[128,512]{0,1:T(8,128)} async-done(((f32[128,512]{0,1:T(8,128)}), f32[128,512]{0,1:T(8,128)}) %all-reduce.21.cloned.1.call-update) | async-done | bytes 262160 | tf_op jit(solution)/shard_map/psum | solution.py:23
  1657.5 1.3 fusion.19
  1658.8 5.3 bitcast_subtract_fusion.1
  1664.1 1.8 copy-done.3
  1665.9 3.7 convolution_bitcast_fusion
  1669.7 0.0 all-reduce.23.cloned.1.call-update
  1669.7 177.1 %all-reduce.23.cloned.1.call-done = f32[128,512]{0,1:T(8,128)} async-done(((f32[128,512]{0,1:T(8,128)}), f32[128,512]{0,1:T(8,128)}) %all-reduce.23.cloned.1.call-update) | async-done | bytes 262160 | tf_op jit(solution)/shard_map/psum | solution.py:23
  1846.8 1.3 fusion.17
  1848.1 6.0 bitcast_subtract_fusion
  1854.1 5.1 copy.5
  (17 shorter events, 0.1 us)
Async XLA Ops:
  6.5 83.5 %all-gather.9.cloned.1.call-start = ((), (), s32[]{:S(2)}) async-start(), calls=%async_computation.8 | async-start | bytes 1949696 | tf_op jit(solution)/shard_map/all_gather | solution.py:33
  8.4 270.9 %all-reduce.9.cloned.1.call-start = ((), (), s32[]{:S(2)}) async-start(), calls=%async_computation | async-start | bytes 524288 | tf_op jit(solution)/shard_map/psum | solution.py:23
  95.2 184.1 %copy-start.8 = (f32[4,2,128,128]{3,2,1,0:T(8,128)S(1)}, f32[4,2,128,128]{3,2,1,0:T(8,128)}, u32[]{:S(2)}) copy-start(f32[4,2,128,128]{3,2,1,0:T(8,128)} %param.5) | copy-start | bytes 1572868
  95.2 185.6 %copy-start.6 = (f32[1,1792,256]{1,2,0:T(8,128)S(1)}, f32[1,1792,256]{1,2,0:T(8,128)}, u32[]{:S(2)}) copy-start(f32[1,1792,256]{1,2,0:T(8,128)} %all-gather.9.cloned.1.call-done) | copy-start | bytes 5505028
  95.3 373.6 %all-reduce.11.cloned.1.call-start = ((), (), s32[]{:S(2)}) async-start(), calls=%async_computation.1 | async-start | bytes 524288 | tf_op jit(solution)/shard_map/psum | solution.py:23
  286.1 1.8 copy-start.1
  291.7 256.6 %all-gather.11.cloned.1.call-start = ((), (), s32[]{:S(2)}) async-start(), calls=%async_computation.9 | async-start | bytes 1949696 | tf_op jit(solution)/shard_map/all_gather | solution.py:33
  292.3 446.5 %all-reduce.13.cloned.1.call-start = ((), (), s32[]{:S(2)}) async-start(), calls=%async_computation.2 | async-start | bytes 524288 | tf_op jit(solution)/shard_map/psum | solution.py:23
  548.4 191.7 %copy-start.5 = (f32[1,1792,256]{1,2,0:T(8,128)S(1)}, f32[1,1792,256]{1,2,0:T(8,128)}, u32[]{:S(2)}) copy-start(f32[1,1792,256]{1,2,0:T(8,128)} %all-gather.11.cloned.1.call-done) | copy-start | bytes 5505028
  554.5 373.7 %all-reduce.15.cloned.1.call-start = ((), (), s32[]{:S(2)}) async-start(), calls=%async_computation.3 | async-start | bytes 524288 | tf_op jit(solution)/shard_map/psum | solution.py:23
  745.4 1.8 copy-start.2
  751.0 256.9 %all-gather.13.cloned.1.call-start = ((), (), s32[]{:S(2)}) async-start(), calls=%async_computation.10 | async-start | bytes 1949696 | tf_op jit(solution)/shard_map/all_gather | solution.py:33
  751.8 446.4 %all-reduce.17.cloned.1.call-start = ((), (), s32[]{:S(2)}) async-start(), calls=%async_computation.4 | async-start | bytes 524288 | tf_op jit(solution)/shard_map/psum | solution.py:23
  1007.9 191.6 %copy-start.4 = (f32[1,1792,256]{1,2,0:T(8,128)S(1)}, f32[1,1792,256]{1,2,0:T(8,128)}, u32[]{:S(2)}) copy-start(f32[1,1792,256]{1,2,0:T(8,128)} %all-gather.13.cloned.1.call-done) | copy-start | bytes 5505028
  1014.1 373.5 %all-reduce.19.cloned.1.call-start = ((), (), s32[]{:S(2)}) async-start(), calls=%async_computation.5 | async-start | bytes 524288 | tf_op jit(solution)/shard_map/psum | solution.py:23
  1204.8 1.8 copy-start
  1210.4 256.7 %all-gather.15.cloned.1.call-start = ((), (), s32[]{:S(2)}) async-start(), calls=%async_computation.11 | async-start | bytes 1949696 | tf_op jit(solution)/shard_map/all_gather | solution.py:33
  1211.0 446.4 %all-reduce.21.cloned.1.call-start = ((), (), s32[]{:S(2)}) async-start(), calls=%async_computation.6 | async-start | bytes 524288 | tf_op jit(solution)/shard_map/psum | solution.py:23
  1467.2 191.6 %copy-start.7 = (f32[1,1792,256]{1,2,0:T(8,128)S(1)}, f32[1,1792,256]{1,2,0:T(8,128)}, u32[]{:S(2)}) copy-start(f32[1,1792,256]{1,2,0:T(8,128)} %all-gather.15.cloned.1.call-done) | copy-start | bytes 5505028
  1473.3 373.5 %all-reduce.23.cloned.1.call-start = ((), (), s32[]{:S(2)}) async-start(), calls=%async_computation.7 | async-start | bytes 524288 | tf_op jit(solution)/shard_map/psum | solution.py:23
  1664.1 1.8 copy-start.3
Sparse Core Ops, SparseCore 0:
  9.1 80.8 all-gather.8
  95.4 183.8 all-reduce.8
  291.9 176.9 all-reduce.10
  470.5 77.8 all-gather.10
  554.7 184.0 all-reduce.12
  751.1 177.0 all-reduce.14
  930.0 77.8 all-gather.12
  1014.2 183.9 all-reduce.16
  1210.5 177.0 all-reduce.18
  1389.3 77.8 all-gather.14
  1473.4 183.9 all-reduce.20
  1669.8 176.9 all-reduce.22
where the time goes:
time: 1870 us
  waiting for transfers between devices  1740 us (93%)
  matrix products  94.3 us (5%)
  local copies, waits for them, and re-layouts  19.6 us (1%)
    psum x8, waiting for transfers between devices, apply_block(): summed = lax.psum(partial_value, 'row')  1440 us
    all_gather x4, waiting for transfers between devices, per_device(): reflectors = lax.all_gather(householder[window], 'col', axis=1, tiled=True)  298 us
    dot_general x16, matrix products, precise_dot(): jnp.dot(left, right, precision=lax.Precision.HIGHEST, preferred_element_t...  55.8 us
    dot_general x8, matrix products, rows_product(): lax.dot_general(left, right, (((0,), (0,)), ((), ())), precision=lax.Prec...  38.5 us
  transfers between devices with their start and end apart: 12, of which 12 were waited for; matrix products, arithmetic and copies ran while one was open for 1% of the time, Pallas kernels for 0%

commit v1 on v0

v1 whole, which is shorter than its diff:
```python
import functools
import jax
import jax.numpy as jnp
from jax import lax
from jax.experimental import pallas as pl
from jax.experimental.pallas import tpu as pltpu
from jax.sharding import PartitionSpec as P

MESH = pl.DeviceIdType.MESH
F32 = jnp.float32
BF16 = jnp.bfloat16
NT = (((1,), (1,)), ((), ()))
NN = (((1,), (0,)), ((), ()))
BLOCKS = 4
K = 256
PANEL = 128
ROWS = 1792
COLS = 512
HALF = COLS // 2
PIECE = HALF // 4
OWN = 16
RUN = 4 * OWN
C_HALF = PANEL // 2


def split(value):
    high = value.astype(BF16)
    low = (value - high.astype(F32)).astype(BF16)
    return high, low


def dot(a, b, dims):
    return lax.dot_general(a, b, dims, preferred_element_type=F32)


def dot3(a_high, a_low, b_high, b_low, dims):
    small = dot(a_low, b_high, dims) + dot(a_high, b_low, dims)
    return dot(a_high, b_high, dims) + small


def exact(a, b, dims):
    return lax.dot_general(
        a, b, dims, precision=lax.Precision.HIGHEST, preferred_element_type=F32
    )


def kernel(
    z_ref, w_ref, t_ref, out_ref,
    zs, zt, zh, zl, wt, wh, wl, tf,
    pt, rc, rx, ps, rz, cp, cc, cx, cs, cz, cf, st,
    local_sem, zg_s, zg_r, yg_s, yg_r, fg_s, fg_r,
    pc_s, pc_r, px_s, px_r, pz_s, pz_r,
    cc_s, cc_r, cx_s, cx_r, cz_s, cz_r, cf_s, cf_r,
    sx_s, sx_r, sc_s, sc_r,
):
    row, col = lax.axis_index("row"), lax.axis_index("col")
    z_hi, x, core = row // 8, (row // 2) % 4, row % 2
    y, z_lo = col // 4, col % 4

    def at_row(hi, xx, cc_):
        return (hi * 8 + xx * 2 + cc_, col)

    def at_col(yy, zz):
        return (row, yy * 4 + zz)

    sibling = at_row(z_hi, x, 1 - core)
    across = at_row(1 - z_hi, x, core)
    x_peers = [at_row(z_hi, (x + d) % 4, core) for d in (1, 2, 3)]
    z_peers = [at_col(y, (z_lo + d) % 4) for d in (1, 2, 3)]
    y_up, y_down = (y + 1) % 4, (y + 3) % 4
    y_peers = [at_col(y_up, z_lo), at_col(y_down, z_lo)]

    own_rows = pl.ds(pl.multiple_of(col * OWN, OWN), OWN)
    run_rows = pl.ds(pl.multiple_of(y * RUN, RUN), RUN)
    first_half = pl.ds(pl.multiple_of(y_down * RUN, RUN), RUN // 2)
    last_half = pl.ds(pl.multiple_of(y_up * RUN + RUN // 2, RUN // 2), RUN // 2)
    mine = pl.multiple_of(core * HALF, HALF)
    theirs = pl.multiple_of((1 - core) * HALF, HALF)
    piece_rows = pl.ds(pl.multiple_of(mine + x * PIECE, PIECE), PIECE)
    c_mine = pl.ds(pl.multiple_of(core * C_HALF, C_HALF), C_HALF)
    c_theirs = pl.ds(pl.multiple_of((1 - core) * C_HALF, C_HALF), C_HALF)

    sent = []

    def send(src, dst, send_sem, recv_sem, device):
        copy = pltpu.make_async_remote_copy(
            src_ref=src, dst_ref=dst, send_sem=send_sem, recv_sem=recv_sem,
            device_id=device, device_id_type=MESH,
        )
        copy.start()
        sent.append(copy)
        return copy

    fetch_z = pltpu.make_async_copy(z_ref, zs, local_sem.at[0])
    fetch_z.start()
    fetch_t = pltpu.make_async_copy(t_ref, tf, local_sem.at[1])
    fetch_t.start()
    fetch_w = []
    for b in range(BLOCKS):
        copy = pltpu.make_async_copy(w_ref.at[b], wt.at[b, own_rows], local_sem.at[2 + b])
        copy.start()
        fetch_w.append(copy)

    barrier = pltpu.get_barrier_semaphore()
    peers = [sibling, across] + x_peers + z_peers + y_peers
    for peer in peers:
        pl.semaphore_signal(barrier, inc=1, device_id=peer, device_id_type=MESH)
    pl.semaphore_wait(barrier, len(peers))

    gather_z, gather_y, gather_f = {}, {}, {}

    def z_send(b):
        gather_z[b] = [
            send(w_ref.at[b], wt.at[b, own_rows], zg_s.at[b, d], zg_r.at[b, d], z_peers[d])
            for d in range(3)
        ]

    def y_send(b):
        fetch_w[b].wait()
        for copy in gather_z[b]:
            copy.wait_recv()
        run = wt.at[b, run_rows]
        gather_y[b] = [
            send(run, run, yg_s.at[b, d], yg_r.at[b, d], y_peers[d]) for d in range(2)
        ]

    def f_send(b):
        up, down = gather_y[b]
        up.wait_recv()
        part = wt.at[b, first_half]
        one = send(part, part, fg_s.at[b, 0], fg_r.at[b, 0], y_peers[0])
        down.wait_recv()
        part = wt.at[b, last_half]
        two = send(part, part, fg_s.at[b, 1], fg_r.at[b, 1], y_peers[1])
        gather_f[b] = [one, two]

    def arrive(b):
        for copy in gather_f[b]:
            copy.wait_recv()

    z_send(0)

    fetch_z.wait()

    @pl.loop(0, ROWS // 128)
    def _(i):
        at = pl.ds(pl.multiple_of(i * 128, 128), 128)
        turned = zs[at, :].T
        zt[:, at] = turned
        zh[:, at], zl[:, at] = split(turned)

    y_send(0)
    z_send(1)
    f_send(0)
    fetch_t.wait()

    def project(b, start):
        at = pl.ds(start, HALF)
        pt[b, at, :] = dot3(zh[at, :], zl[at, :], wh[...], wl[...], NT)

    def update(b, start):
        at = pl.ds(start, HALF)
        s_high, s_low = split(st[b, at, :])

        @pl.loop(0, ROWS // K)
        def _(i):
            lanes = pl.ds(pl.multiple_of(i * K, K), K)
            fresh = zt[at, lanes] - dot3(s_high, s_low, wh[:, lanes], wl[:, lanes], NN)
            zt[at, lanes] = fresh
            zh[at, lanes], zl[at, lanes] = split(fresh)

    for b in range(BLOCKS):
        arrive(b)

        @pl.loop(0, ROWS // K)
        def _(i):
            lanes = pl.ds(pl.multiple_of(i * K, K), K)
            wh[:, lanes], wl[:, lanes] = split(wt[b, :, lanes])

        cp[b] = dot3(wh[PANEL:, :], wl[PANEL:, :], wh[:PANEL, :], wl[:PANEL, :], NT)
        c_core = send(cp.at[b, c_theirs], cc.at[b], cc_s.at[b], cc_r.at[b], sibling)
        project(b, theirs)
        p_core = send(
            pt.at[b, pl.ds(theirs, HALF)], rc.at[b], pc_s.at[b], pc_r.at[b], sibling
        )
        c_core.wait_recv()
        cp[b, c_mine, :] = cp[b, c_mine, :] + cc[b]
        c_x = [
            send(cp.at[b, c_mine], cx.at[b, d], cx_s.at[b, d], cx_r.at[b, d], x_peers[d])
            for d in range(3)
        ]
        project(b, mine)
        p_core.wait_recv()
        at = pl.ds(mine, HALF)
        pt[b, at, :] = pt[b, at, :] + rc[b]
        p_x = []
        for d in range(3):
            to = pl.multiple_of(mine + ((x + 1 + d) % 4) * PIECE, PIECE)
            p_x.append(
                send(
                    pt.at[b, pl.ds(to, PIECE)], rx.at[b, d],
                    px_s.at[b, d], px_r.at[b, d], x_peers[d],
                )
            )
        if b + 1 < BLOCKS:
            y_send(b + 1)
        if b + 2 < BLOCKS:
            z_send(b + 2)
        for copy in c_x:
            copy.wait_recv()
        cs[b] = (cp[b, c_mine, :] + cx[b, 0]) + (cx[b, 1] + cx[b, 2])
        c_z = send(cs.at[b], cz.at[b], cz_s.at[b], cz_r.at[b], across)
        for copy in p_x:
            copy.wait_recv()
        ps[b] = (pt[b, piece_rows, :] + rx[b, 0]) + (rx[b, 1] + rx[b, 2])
        p_z = send(ps.at[b], rz.at[b], pz_s.at[b], pz_r.at[b], across)
        c_z.wait_recv()
        cf[b, c_mine, :] = cs[b] + cz[b]
        c_f = send(cf.at[b, c_mine], cf.at[b, c_mine], cf_s.at[b], cf_r.at[b], sibling)
        if b + 1 < BLOCKS:
            f_send(b + 1)
        p_z.wait_recv()
        total = ps[b] + rz[b]
        tail = exact(total[:, PANEL:], tf[b, 1], NT)
        c_f.wait_recv()
        lead = exact(total[:, :PANEL] - exact(tail, cf[b], NN), tf[b, 0], NT)
        st[b, piece_rows, :PANEL] = lead
        st[b, piece_rows, PANEL:] = tail
        s_x = [
            send(
                st.at[b, piece_rows], st.at[b, piece_rows],
                sx_s.at[b, d], sx_r.at[b, d], x_peers[d],
            )
            for d in range(3)
        ]
        for copy in s_x:
            copy.wait_recv()
        part = st.at[b, pl.ds(mine, HALF)]
        s_core = send(part, part, sc_s.at[b], sc_r.at[b], sibling)
        update(b, mine)
        s_core.wait_recv()
        update(b, theirs)

    store = pltpu.make_async_copy(zt, out_ref, local_sem.at[0])
    store.start()
    for copy in sent:
        copy.wait_send()
    store.wait()


def per_device(eigvec, householder, panel_factors):
    dma = pltpu.SemaphoreType.DMA
    n = BLOCKS
    scratch = [
        pltpu.VMEM((ROWS, COLS), F32),
        pltpu.VMEM((COLS, ROWS), F32),
        pltpu.VMEM((COLS, ROWS), BF16),
        pltpu.VMEM((COLS, ROWS), BF16),
        pltpu.VMEM((n, K, ROWS), F32),
        pltpu.VMEM((K, ROWS), BF16),
        pltpu.VMEM((K, ROWS), BF16),
        pltpu.VMEM((n, 2, PANEL, PANEL), F32),
        pltpu.VMEM((n, COLS, K), F32),
        pltpu.VMEM((n, HALF, K), F32),
        pltpu.VMEM((n, 3, PIECE, K), F32),
        pltpu.VMEM((n, PIECE, K), F32),
        pltpu.VMEM((n, PIECE, K), F32),
        pltpu.VMEM((n, PANEL, PANEL), F32),
        pltpu.VMEM((n, C_HALF, PANEL), F32),
        pltpu.VMEM((n, 3, C_HALF, PANEL), F32),
        pltpu.VMEM((n, C_HALF, PANEL), F32),
        pltpu.VMEM((n, C_HALF, PANEL), F32),
        pltpu.VMEM((n, PANEL, PANEL), F32),
        pltpu.VMEM((n, COLS, K), F32),
        dma((2 + n,)),
        dma((n, 3)), dma((n, 3)), dma((n, 2)), dma((n, 2)), dma((n, 2)), dma((n, 2)),
        dma((n,)), dma((n,)), dma((n, 3)), dma((n, 3)), dma((n,)), dma((n,)),
        dma((n,)), dma((n,)), dma((n, 3)), dma((n, 3)), dma((n,)), dma((n,)), dma((n,)), dma((n,)),
        dma((n, 3)), dma((n, 3)), dma((n,)), dma((n,)),
    ]
    turned = pl.pallas_call(
        kernel,
        out_shape=jax.ShapeDtypeStruct((COLS, ROWS), F32),
        in_specs=[pl.BlockSpec(memory_space=pl.ANY)] * 3,
        out_specs=pl.BlockSpec(memory_space=pl.ANY),
        scratch_shapes=scratch,
        compiler_params=pltpu.CompilerParams(
            collective_id=0, has_side_effects=True, vmem_limit_bytes=56 << 20
        ),
        cost_estimate=pl.CostEstimate(
            flops=2 * 2 * 3 * n * K * ROWS * COLS, bytes_accessed=8 << 20, transcendentals=0
        ),
        name="back_transform",
    )(eigvec, jnp.transpose(householder, (0, 2, 1)), panel_factors)
    return turned.T


def solution(mesh):
    in_specs = (P("row", "col"), P(None, "row", "col"), P())
    out_specs = P("row", "col")
    return jax.shard_map(
        per_device, mesh=mesh, in_specs=in_specs, out_specs=out_specs, check_vma=False
    )
```

time: 1870 us -> 156 us (0.08)
  waiting for transfers between devices: 1740 us -> 0 us
  Pallas kernels: 0 us -> 150 us
  matrix products: 94.3 us -> 0 us
    psum x8 -> x0, waiting for transfers between devices: 1440 us -> none  [apply_block(): summed = lax.psum(partial_value, 'row')]
    all_gather x4 -> x0, waiting for transfers between devices: 298 us -> none  [per_device(): reflectors = lax.all_gather(householder[window], 'col', axis=1, tiled=True)]
    pallas_call x0 -> x1, Pallas kernels: none -> 150 us  [per_device(): pl.pallas_call(kernel, out_shape=jax.ShapeDtypeStruct((COLS, ROWS), F32),...]
    dot_general x24 -> x0, matrix products: 94.3 us -> none  [the longest x16 55.8 us: precise_dot(): jnp.dot(left, right, precision=lax.Precision.HIGHEST, preferred_element_t...]
  transfers between devices with their start and end apart: 12 -> 0, of which waited for: 12 -> 0; matrix products, arithmetic and copies ran while one was open for 1% -> 0% of each run, Pallas kernels for 0% -> 0%
where the time goes in v1:
time: 156 us
  Pallas kernels  150 us (96%)
  local copies, waits for them, and re-layouts  5.12 us (3%)
    pallas_call x1, Pallas kernels, per_device(): pl.pallas_call(kernel, out_shape=jax.ShapeDtypeStruct((COLS, ROWS), F32),...  150 us
    transpose x1, local copies, waits for them, and re-layouts, per_device(): return turned.T  5.12 us

profile of v1, /device:TPU:1, one launch (start us, length us, event | category | flops | bytes accessed | tf_op | source)
XLA Modules:
  0.0 155.6 jit_solution(5564621805011831544)
XLA Ops:
  0.0 150.5 %back_transform.1 = f32[512,1792]{1,0:T(8,128)} custom-call(f32[1792,512]{1,0:T(8,128)} %z_ref.1, f32[4,16,1792]{2,1,0:T(8,128)} %bitcast.3, f32[4,2,128,128]{3,2,1,0:T(8,128)} %t_ref.1), custom_call_target="tpu_custom_call" | custom-call | flops 11274289152 | bytes 8388608 | tf_op jit(solution)/shard_map/back_transform/pallas_call | solution.py:281
  150.5 5.1 %copy.4 = f32[1792,512]{1,0:T(8,128)} copy(f32[1792,512]{0,1:T(8,128)} %bitcast.2) | data formatting | bytes 7340032 | tf_op jit(solution)/shard_map/transpose | solution.py:295

commit v2 on v1

v2 whole, which is shorter than its diff:
```python
import functools
import jax
import jax.numpy as jnp
from jax import lax
from jax.experimental import pallas as pl
from jax.experimental.pallas import tpu as pltpu
from jax.sharding import PartitionSpec as P

MESH = pl.DeviceIdType.MESH
F32 = jnp.float32
BF16 = jnp.bfloat16
NT = (((1,), (1,)), ((), ()))
NN = (((1,), (0,)), ((), ()))
BLOCKS = 4
K = 256
PANEL = 128
ROWS = 1792
COLS = 512
HALF = COLS // 2
PIECE = HALF // 4
UNITS = 2 * BLOCKS
RUN = 64
WIDE = (BLOCKS - 1) * K
C_HALF = PANEL // 2
ORDER = (
    "z0", "z1", "t0", "y0", "z2", "y1", "z3", "y0", "y2", "z4", "y1", "y3", "z5", "y0", "y2",
    "y4", "z6", "y1", "g1", "c0", "p0", "g1", "c0", "p0", "y3", "y5", "z7", "g1", "y2", "c0",
    "p0", "y4", "y6", "g1", "y3", "g2", "c1", "c0", "p1", "g2", "y5", "y7", "c0", "p0", "s0",
    "p1", "c1", "y4", "g2", "s0", "y6", "g1", "g2", "s0", "y5", "g3", "p1", "c2", "c1", "p2",
    "y7", "g3", "c2", "p2", "y6", "g1", "g2", "g3", "y7", "g2", "c3", "c2", "c1", "p3", "p2",
    "c3", "p3", "g3", "g1", "g1", "c1", "p1", "s1", "g3", "c2", "g2", "c3", "g2", "g3", "c2",
    "p2", "s2", "p3", "s1", "c3", "s1", "g3", "g3", "c3", "p3", "s3", "s2", "s2", "s3", "s3",
)


def split(value):
    high = value.astype(BF16)
    low = (value - high.astype(F32)).astype(BF16)
    return high, low


def dot(a, b, dims):
    return lax.dot_general(a, b, dims, preferred_element_type=F32)


def dot3(a_high, a_low, b_high, b_low, dims):
    small = dot(a_low, b_high, dims) + dot(a_high, b_low, dims)
    return dot(a_high, b_high, dims) + small


def exact(a, b, dims):
    return lax.dot_general(
        a, b, dims, precision=lax.Precision.HIGHEST, preferred_element_type=F32
    )


def kernel(
    z_ref, w_ref, t_ref, out_ref,
    zs, zt, zh, zl, wt, wh, wl, tf,
    pt, rc, rx, ps, rz, cp, cc, cx, cs, cz, cf, gp, gc, gx, gs, gz, gt, fix, st,
    local_sem, zg_s, zg_r, yg_s, yg_r, fg_s, fg_r,
    pc_s, pc_r, px_s, px_r, pz_s, pz_r,
    cc_s, cc_r, cx_s, cx_r, cz_s, cz_r, cf_s, cf_r,
    gc_s, gc_r, gx_s, gx_r, gz_s, gz_r, gy_s, gy_r, gf_s, gf_r, ga_s, ga_r, ge_s, ge_r,
    sx_s, sx_r, sc_s, sc_r,
):
    row, col = lax.axis_index("row"), lax.axis_index("col")
    z_hi, x, core = row // 8, (row // 2) % 4, row % 2
    y, z_lo = col // 4, col % 4

    def at_row(hi, xx, cc_):
        return (hi * 8 + xx * 2 + cc_, col)

    def at_col(yy, zz):
        return (row, yy * 4 + zz)

    sibling = at_row(z_hi, x, 1 - core)
    across = at_row(1 - z_hi, x, core)
    x_peers = [at_row(z_hi, (x + d) % 4, core) for d in (1, 2, 3)]
    z_peers = [at_col(y, (z_lo + d) % 4) for d in (1, 2, 3)]
    y_up, y_down = (y + 1) % 4, (y + 3) % 4
    y_peers = [at_col(y_up, z_lo), at_col(y_down, z_lo)]

    mine = pl.multiple_of(core * HALF, HALF)
    theirs = pl.multiple_of((1 - core) * HALF, HALF)
    piece_rows = pl.ds(pl.multiple_of(mine + x * PIECE, PIECE), PIECE)
    c_mine = pl.ds(pl.multiple_of(core * C_HALF, C_HALF), C_HALF)
    c_theirs = pl.ds(pl.multiple_of((1 - core) * C_HALF, C_HALF), C_HALF)

    sent = []

    def send(src, dst, send_sem, recv_sem, device):
        copy = pltpu.make_async_remote_copy(
            src_ref=src, dst_ref=dst, send_sem=send_sem, recv_sem=recv_sem,
            device_id=device, device_id_type=MESH,
        )
        copy.start()
        sent.append(copy)
        return copy

    def received(copies):
        for copy in copies:
            copy.wait_recv()

    fetch_w = []
    for b in range(BLOCKS):
        copy = pltpu.make_async_copy(w_ref.at[b], wt.at[b, col], local_sem.at[2 + b])
        copy.start()
        fetch_w.append(copy)
    fetch_z = pltpu.make_async_copy(z_ref, zs, local_sem.at[0])
    fetch_z.start()
    fetch_t = pltpu.make_async_copy(t_ref, tf, local_sem.at[1])
    fetch_t.start()

    barrier = pltpu.get_barrier_semaphore()
    peers = [sibling, across] + x_peers + z_peers + y_peers
    for peer in peers:
        pl.semaphore_signal(barrier, inc=1, device_id=peer, device_id_type=MESH)
    pl.semaphore_wait(barrier, len(peers))

    def weights(b):
        @pl.loop(0, ROWS // K)
        def _(i):
            lanes = pl.ds(pl.multiple_of(i * K, K), K)
            both = wt[b, :, :, :, lanes].reshape(K, K)
            wh[b, :, lanes], wl[b, :, lanes] = split(both)

    def project(b, start):
        at = pl.ds(start, HALF)
        pt[b, at, :] = dot3(zh[at, :], zl[at, :], wh[b], wl[b], NT)

    def update(b, start):
        at = pl.ds(start, HALF)
        s_high, s_low = split(st[b, at, :])

        @pl.loop(0, ROWS // K)
        def _(i):
            lanes = pl.ds(pl.multiple_of(i * K, K), K)
            zt[at, lanes] -= dot3(s_high, s_low, wh[b, :, lanes], wl[b, :, lanes], NN)

    gathered = [None] * UNITS

    def z_flow(u):
        b, h = u // 2, u % 2
        gathered[u] = [
            send(w_ref.at[b, h], wt.at[b, col, h], zg_s.at[u, d], zg_r.at[u, d], z_peers[d])
            for d in range(3)
        ]
        yield

    def y_flow(u):
        b, h = u // 2, u % 2
        if h == 0:
            fetch_w[b].wait()
        received(gathered[u])
        run = wt.at[b, pl.ds(4 * y, 4), h]
        up, down = [
            send(run, run, yg_s.at[u, d], yg_r.at[u, d], y_peers[d]) for d in range(2)
        ]
        yield
        up.wait_recv()
        part = wt.at[b, pl.ds(4 * y_down, 2), h]
        one = send(part, part, fg_s.at[u, 0], fg_r.at[u, 0], y_peers[0])
        down.wait_recv()
        part = wt.at[b, pl.ds(4 * y_up + 2, 2), h]
        two = send(part, part, fg_s.at[u, 1], fg_r.at[u, 1], y_peers[1])
        yield
        received([one, two])
        if h == 1:
            weights(b)
        yield

    def c_flow(b):
        cp[b] = dot3(wh[b, PANEL:, :], wl[b, PANEL:, :], wh[b, :PANEL, :], wl[b, :PANEL, :], NT)
        to_core = send(cp.at[b, c_theirs], cc.at[b], cc_s.at[b], cc_r.at[b], sibling)
        yield
        to_core.wait_recv()
        cp[b, c_mine, :] = cp[b, c_mine, :] + cc[b]
        to_x = [
            send(cp.at[b, c_mine], cx.at[b, d], cx_s.at[b, d], cx_r.at[b, d], x_peers[d])
            for d in range(3)
        ]
        yield
        received(to_x)
        cs[b] = (cp[b, c_mine, :] + cx[b, 0]) + (cx[b, 1] + cx[b, 2])
        to_z = send(cs.at[b], cz.at[b], cz_s.at[b], cz_r.at[b], across)
        yield
        to_z.wait_recv()
        cf[b, c_mine, :] = cs[b] + cz[b]
        part = cf.at[b, c_mine]
        to_core = send(part, part, cf_s.at[b], cf_r.at[b], sibling)
        yield
        to_core.wait_recv()
        yield

    def p_flow(b):
        project(b, theirs)
        to_core = send(
            pt.at[b, pl.ds(theirs, HALF)], rc.at[b], pc_s.at[b], pc_r.at[b], sibling
        )
        project(b, mine)
        yield
        to_core.wait_recv()
        at = pl.ds(mine, HALF)
        pt[b, at, :] = pt[b, at, :] + rc[b]
        to_x = []
        for d in range(3):
            to = pl.multiple_of(mine + ((x + 1 + d) % 4) * PIECE, PIECE)
            to_x.append(
                send(
                    pt.at[b, pl.ds(to, PIECE)], rx.at[b, d],
                    px_s.at[b, d], px_r.at[b, d], x_peers[d],
                )
            )
        yield
        received(to_x)
        ps[b] = (pt[b, piece_rows, :] + rx[b, 0]) + (rx[b, 1] + rx[b, 2])
        to_z = send(ps.at[b], rz.at[b], pz_s.at[b], pz_r.at[b], across)
        yield
        to_z.wait_recv()
        yield

    def g_flow(b):
        g, wide = b - 1, b * K
        own = wt[b, pl.ds(4 * y, 4)].reshape(RUN, ROWS)
        own_high, own_low = split(own)
        for c in range(b):
            gp[g, :, c * K : (c + 1) * K] = dot3(own_high, own_low, wh[c], wl[c], NT)
        lanes = pl.ds(0, wide)
        base = pl.multiple_of(core * 32, 32)
        other = pl.multiple_of((1 - core) * 32, 32)
        to_core = send(
            gp.at[g, pl.ds(other, 32), lanes], gc.at[g, :, lanes], gc_s.at[g], gc_r.at[g], sibling
        )
        yield
        to_core.wait_recv()
        at = pl.ds(base, 32)
        gp[g, at, :wide] = gp[g, at, :wide] + gc[g, :, :wide]
        to_x = []
        for d in range(3):
            to = pl.multiple_of(base + ((x + 1 + d) % 4) * 8, 8)
            to_x.append(
                send(
                    gp.at[g, pl.ds(to, 8), lanes], gx.at[g, d, :, lanes],
                    gx_s.at[g, d], gx_r.at[g, d], x_peers[d],
                )
            )
        yield
        received(to_x)
        at = pl.ds(pl.multiple_of(base + x * 8, 8), 8)
        gs[g, :, :wide] = (gp[g, at, :wide] + gx[g, 0, :, :wide]) + (
            gx[g, 1, :, :wide] + gx[g, 2, :, :wide]
        )
        to_z = send(
            gs.at[g, :, lanes], gz.at[g, :, lanes], gz_s.at[g], gz_r.at[g], across
        )
        yield
        to_z.wait_recv()
        gt[g, y, core, x, :, :wide] = gs[g, :, :wide] + gz[g, :, :wide]
        part = gt.at[g, y, core, x, :, lanes]
        up, down = [
            send(part, part, gy_s.at[g, d], gy_r.at[g, d], y_peers[d]) for d in range(2)
        ]
        yield
        up.wait_recv()
        part = gt.at[g, y_down, core, x, :, pl.ds(0, wide // 2)]
        one = send(part, part, gf_s.at[g, 0], gf_r.at[g, 0], y_peers[0])
        down.wait_recv()
        part = gt.at[g, y_up, core, x, :, pl.ds(wide // 2, wide // 2)]
        two = send(part, part, gf_s.at[g, 1], gf_r.at[g, 1], y_peers[1])
        yield
        received([one, two])
        part = gt.at[g, :, core, x, :, lanes]
        to_x = [
            send(part, part, ga_s.at[g, d], ga_r.at[g, d], x_peers[d]) for d in range(3)
        ]
        yield
        received(to_x)
        part = gt.at[g, :, core, :, :, lanes]
        to_core = send(part, part, ge_s.at[g], ge_r.at[g], sibling)
        yield
        to_core.wait_recv()
        total = None
        for c in range(b):
            seen = gt[g, :, :, :, :, c * K : (c + 1) * K].reshape(K, K)
            term = exact(st[c, piece_rows, :], seen, NT)
            total = term if total is None else total + term
        fix[g] = total
        yield

    def s_flow(b):
        total = ps[b] + rz[b]
        if b:
            total = total - fix[b - 1]
        tail = exact(total[:, PANEL:], tf[b, 1], NT)
        lead = exact(total[:, :PANEL] - exact(tail, cf[b], NN), tf[b, 0], NT)
        st[b, piece_rows, :PANEL] = lead
        st[b, piece_rows, PANEL:] = tail
        part = st.at[b, piece_rows]
        to_x = [
            send(part, part, sx_s.at[b, d], sx_r.at[b, d], x_peers[d]) for d in range(3)
        ]
        yield
        received(to_x)
        part = st.at[b, pl.ds(mine, HALF)]
        to_core = send(part, part, sc_s.at[b], sc_r.at[b], sibling)
        if b == BLOCKS - 1:
            update(b, mine)
        yield
        to_core.wait_recv()
        if b < BLOCKS - 1:
            update(b, mine)
        update(b, theirs)
        yield

    def start(_):
        fetch_t.wait()
        fetch_z.wait()

        @pl.loop(0, ROWS // 128)
        def _(i):
            at = pl.ds(pl.multiple_of(i * 128, 128), 128)
            turned = zs[at, :].T
            zt[:, at] = turned
            zh[:, at], zl[:, at] = split(turned)

        yield

    flows = {"t": start, "z": z_flow, "y": y_flow, "c": c_flow, "p": p_flow, "g": g_flow, "s": s_flow}
    steps = {}
    for name in ORDER:
        if name not in steps:
            steps[name] = flows[name[0]](int(name[1:]))
        next(steps[name])

    store = pltpu.make_async_copy(zt, out_ref, local_sem.at[0])
    store.start()
    for copy in sent:
        copy.wait_send()
    store.wait()


def per_device(eigvec, householder, panel_factors):
    dma = pltpu.SemaphoreType.DMA
    n, g = BLOCKS, BLOCKS - 1
    scratch = [
        pltpu.VMEM((ROWS, COLS), F32),
        pltpu.VMEM((COLS, ROWS), F32),
        pltpu.VMEM((COLS, ROWS), BF16),
        pltpu.VMEM((COLS, ROWS), BF16),
        pltpu.VMEM((n, 16, 2, 8, ROWS), F32),
        pltpu.VMEM((n, K, ROWS), BF16),
        pltpu.VMEM((n, K, ROWS), BF16),
        pltpu.VMEM((n, 2, PANEL, PANEL), F32),
        pltpu.VMEM((n, COLS, K), F32),
        pltpu.VMEM((n, HALF, K), F32),
        pltpu.VMEM((n, 3, PIECE, K), F32),
        pltpu.VMEM((n, PIECE, K), F32),
        pltpu.VMEM((n, PIECE, K), F32),
        pltpu.VMEM((n, PANEL, PANEL), F32),
        pltpu.VMEM((n, C_HALF, PANEL), F32),
        pltpu.VMEM((n, 3, C_HALF, PANEL), F32),
        pltpu.VMEM((n, C_HALF, PANEL), F32),
        pltpu.VMEM((n, C_HALF, PANEL), F32),
        pltpu.VMEM((n, PANEL, PANEL), F32),
        pltpu.VMEM((g, RUN, WIDE), F32),
        pltpu.VMEM((g, RUN // 2, WIDE), F32),
        pltpu.VMEM((g, 3, 8, WIDE), F32),
        pltpu.VMEM((g, 8, WIDE), F32),
        pltpu.VMEM((g, 8, WIDE), F32),
        pltpu.VMEM((g, 4, 2, 4, 8, WIDE), F32),
        pltpu.VMEM((g, PIECE, K), F32),
        pltpu.VMEM((n, COLS, K), F32),
        dma((2 + n,)),
    ]
    for shape in (
        (UNITS, 3), (UNITS, 2), (UNITS, 2),
        (n,), (n, 3), (n,),
        (n,), (n, 3), (n,), (n,),
        (g,), (g, 3), (g,), (g, 2), (g, 2), (g, 3), (g,),
        (n, 3), (n,),
    ):
        scratch += [dma(shape), dma(shape)]
    turned = pl.pallas_call(
        kernel,
        out_shape=jax.ShapeDtypeStruct((COLS, ROWS), F32),
        in_specs=[pl.BlockSpec(memory_space=pl.ANY)] * 3,
        out_specs=pl.BlockSpec(memory_space=pl.ANY),
        scratch_shapes=scratch,
        compiler_params=pltpu.CompilerParams(
            collective_id=0, has_side_effects=True, vmem_limit_bytes=58 << 20
        ),
        cost_estimate=pl.CostEstimate(
            flops=2 * 2 * 3 * n * K * ROWS * COLS, bytes_accessed=8 << 20, transcendentals=0
        ),
        name="back_transform",
    )(
        eigvec,
        jnp.transpose(householder, (0, 2, 1)).reshape(n, 2, 8, ROWS),
        panel_factors,
    )
    return turned.T


def solution(mesh):
    in_specs = (P("row", "col"), P(None, "row", "col"), P())
    out_specs = P("row", "col")
    return jax.shard_map(
        per_device, mesh=mesh, in_specs=in_specs, out_specs=out_specs, check_vma=False
    )
```

time: 156 us -> 130 us (0.83)
  Pallas kernels: 150 us -> 124 us
    pallas_call x1, Pallas kernels: 150 us -> 124 us  [per_device(): pl.pallas_call(kernel, out_shape=jax.ShapeDtypeStruct((COLS, ROWS), F32),...]
where the time goes in v2:
time: 130 us; the launch traced here: 129 us
  Pallas kernels  124 us (95%)
  local copies, waits for them, and re-layouts  5.12 us (4%)
    pallas_call x1, Pallas kernels, per_device(): pl.pallas_call(kernel, out_shape=jax.ShapeDtypeStruct((COLS, ROWS), F32),...  124 us
    transpose x1, local copies, waits for them, and re-layouts, per_device(): return turned.T  5.12 us

profile of v2, /device:TPU:1, one launch (start us, length us, event | category | flops | bytes accessed | tf_op | source)
XLA Modules:
  0.0 128.9 jit_solution(17334357630828832688)
XLA Ops:
  0.0 123.7 %back_transform.1 = f32[512,1792]{1,0:T(8,128)} custom-call(f32[1792,512]{1,0:T(8,128)} %z_ref.1, f32[4,2,8,1792]{3,2,1,0:T(8,128)} %bitcast.5, f32[4,2,128,128]{3,2,1,0:T(8,128)} %t_ref.1), custom_call_target="tpu_custom_call" | custom-call | flops 11274289152 | bytes 8388608 | tf_op jit(solution)/shard_map/back_transform/pallas_call | solution.py:384
  123.7 5.1 %copy.4 = f32[1792,512]{1,0:T(8,128)} copy(f32[1792,512]{0,1:T(8,128)} %bitcast.4) | data formatting | bytes 7340032 | tf_op jit(solution)/shard_map/transpose | solution.py:402

commit v3 on v2

--- a/solution.py
+++ b/solution.py
@@ -18,18 +18,23 @@
 COLS = 512
 HALF = COLS // 2
 PIECE = HALF // 4
-UNITS = 2 * BLOCKS
+UNITS = tuple((b, h, 0, ROWS) for b in range(BLOCKS) for h in range(2))
+FIRST = {unit[0]: u for u, unit in reversed(list(enumerate(UNITS)))}
+LAST = {unit[0]: u for u, unit in enumerate(UNITS)}
 RUN = 64
-WIDE = (BLOCKS - 1) * K
+PAIRS = {1: (0,), 2: (1,), 3: (1, 2)}
+APPLIED = 0
+WIDE = 2 * K
 C_HALF = PANEL // 2
 ORDER = (
     "z0", "z1", "t0", "y0", "z2", "y1", "z3", "y0", "y2", "z4", "y1", "y3", "z5", "y0", "y2",
-    "y4", "z6", "y1", "g1", "c0", "p0", "g1", "c0", "p0", "y3", "y5", "z7", "g1", "y2", "c0",
-    "p0", "y4", "y6", "g1", "y3", "g2", "c1", "c0", "p1", "g2", "y5", "y7", "c0", "p0", "s0",
-    "p1", "c1", "y4", "g2", "s0", "y6", "g1", "g2", "s0", "y5", "g3", "p1", "c2", "c1", "p2",
-    "y7", "g3", "c2", "p2", "y6", "g1", "g2", "g3", "y7", "g2", "c3", "c2", "c1", "p3", "p2",
-    "c3", "p3", "g3", "g1", "g1", "c1", "p1", "s1", "g3", "c2", "g2", "c3", "g2", "g3", "c2",
-    "p2", "s2", "p3", "s1", "c3", "s1", "g3", "g3", "c3", "p3", "s3", "s2", "s2", "s3", "s3",
+    "y4", "z6", "y1", "g1", "c0", "p0", "g1", "p0", "c0", "y3", "y5", "z7", "p0", "g1", "y2",
+    "c0", "p0", "y4", "y6", "y3", "g2", "c1", "g1", "c0", "p1", "g2", "c0", "p0", "s0", "p1",
+    "c1", "p1", "y4", "g2", "y5", "y7", "s0", "g2", "c1", "y6", "g1", "s0", "y5", "c2", "g3",
+    "p1", "c2", "y7", "g2", "c1", "p2", "g3", "p2", "y6", "g1", "p2", "c2", "g3", "y7", "p3",
+    "g2", "p3", "g3", "g1", "c2", "p3", "p2", "c3", "g1", "c1", "p1", "s1", "g3", "c3", "g2",
+    "g2", "g3", "p3", "c2", "p2", "s2", "s1", "c3", "s1", "g3", "c3", "g3", "c3", "p3", "s3",
+    "s2", "s2", "s3", "s3",
 )
 
 
@@ -136,37 +141,45 @@
         @pl.loop(0, ROWS // K)
         def _(i):
             lanes = pl.ds(pl.multiple_of(i * K, K), K)
-            zt[at, lanes] -= dot3(s_high, s_low, wh[b, :, lanes], wl[b, :, lanes], NN)
-
-    gathered = [None] * UNITS
+            fresh = zt[at, lanes] - dot3(s_high, s_low, wh[b, :, lanes], wl[b, :, lanes], NN)
+            zt[at, lanes] = fresh
+            if b == APPLIED:
+                zh[at, lanes], zl[at, lanes] = split(fresh)
+
+    gathered = [None] * len(UNITS)
 
     def z_flow(u):
-        b, h = u // 2, u % 2
+        b, h, at, rows = UNITS[u]
+        lanes = pl.ds(at, rows)
         gathered[u] = [
-            send(w_ref.at[b, h], wt.at[b, col, h], zg_s.at[u, d], zg_r.at[u, d], z_peers[d])
+            send(
+                w_ref.at[b, h, :, lanes], wt.at[b, col, h, :, lanes],
+                zg_s.at[u, d], zg_r.at[u, d], z_peers[d],
+            )
             for d in range(3)
         ]
         yield
 
     def y_flow(u):
-        b, h = u // 2, u % 2
-        if h == 0:
+        b, h, at, rows = UNITS[u]
+        lanes = pl.ds(at, rows)
+        if u == FIRST[b]:
             fetch_w[b].wait()
         received(gathered[u])
-        run = wt.at[b, pl.ds(4 * y, 4), h]
+        run = wt.at[b, pl.ds(4 * y, 4), h, :, lanes]
         up, down = [
             send(run, run, yg_s.at[u, d], yg_r.at[u, d], y_peers[d]) for d in range(2)
         ]
         yield
         up.wait_recv()
-        part = wt.at[b, pl.ds(4 * y_down, 2), h]
+        part = wt.at[b, pl.ds(4 * y_down, 2), h, :, lanes]
         one = send(part, part, fg_s.at[u, 0], fg_r.at[u, 0], y_peers[0])
         down.wait_recv()
-        part = wt.at[b, pl.ds(4 * y_up + 2, 2), h]
+        part = wt.at[b, pl.ds(4 * y_up + 2, 2), h, :, lanes]
         two = send(part, part, fg_s.at[u, 1], fg_r.at[u, 1], y_peers[1])
         yield
         received([one, two])
-        if h == 1:
+        if u == LAST[b]:
             weights(b)
         yield
 
@@ -198,6 +211,7 @@
         to_core = send(
             pt.at[b, pl.ds(theirs, HALF)], rc.at[b], pc_s.at[b], pc_r.at[b], sibling
         )
+        yield
         project(b, mine)
         yield
         to_core.wait_recv()
@@ -221,11 +235,11 @@
         yield
 
     def g_flow(b):
-        g, wide = b - 1, b * K
+        g, wide = b - 1, len(PAIRS[b]) * K
         own = wt[b, pl.ds(4 * y, 4)].reshape(RUN, ROWS)
         own_high, own_low = split(own)
-        for c in range(b):
-            gp[g, :, c * K : (c + 1) * K] = dot3(own_high, own_low, wh[c], wl[c], NT)
+        for i, c in enumerate(PAIRS[b]):
+            gp[g, :, i * K : (i + 1) * K] = dot3(own_high, own_low, wh[c], wl[c], NT)
         lanes = pl.ds(0, wide)
         base = pl.multiple_of(core * 32, 32)
         other = pl.multiple_of((1 - core) * 32, 32)
@@ -281,8 +295,8 @@
         yield
         to_core.wait_recv()
         total = None
-        for c in range(b):
-            seen = gt[g, :, :, :, :, c * K : (c + 1) * K].reshape(K, K)
+        for i, c in enumerate(PAIRS[b]):
+            seen = gt[g, :, :, :, :, i * K : (i + 1) * K].reshape(K, K)
             term = exact(st[c, piece_rows, :], seen, NT)
             total = term if total is None else total + term
         fix[g] = total
@@ -374,7 +388,7 @@
         dma((2 + n,)),
     ]
     for shape in (
-        (UNITS, 3), (UNITS, 2), (UNITS, 2),
+        (len(UNITS), 3), (len(UNITS), 2), (len(UNITS), 2),
         (n,), (n, 3), (n,),
         (n,), (n, 3), (n,), (n,),
         (g,), (g, 3), (g,), (g, 2), (g, 2), (g, 3), (g,),

time: 130 us -> 123 us (0.946)
  Pallas kernels: 124 us -> 117 us
    pallas_call x1, Pallas kernels: 124 us -> 117 us  [per_device(): pl.pallas_call(kernel, out_shape=jax.ShapeDtypeStruct((COLS, ROWS), F32),...]
where the time goes in v3:
time: 123 us; the launch traced here: 122 us
  Pallas kernels  117 us (95%)
  local copies, waits for them, and re-layouts  5.12 us (4%)
    pallas_call x1, Pallas kernels, per_device(): pl.pallas_call(kernel, out_shape=jax.ShapeDtypeStruct((COLS, ROWS), F32),...  117 us
    transpose x1, local copies, waits for them, and re-layouts, per_device(): return turned.T  5.12 us

profile of v3, /device:TPU:1, one launch (start us, length us, event | category | flops | bytes accessed | tf_op | source)
XLA Modules:
  0.0 122.3 jit_solution(17990579234994753331)
XLA Ops:
  0.0 117.1 %back_transform.1 = f32[512,1792]{1,0:T(8,128)} custom-call(f32[1792,512]{1,0:T(8,128)} %z_ref.1, f32[4,2,8,1792]{3,2,1,0:T(8,128)} %bitcast.5, f32[4,2,128,128]{3,2,1,0:T(8,128)} %t_ref.1), custom_call_target="tpu_custom_call" | custom-call | flops 11274289152 | bytes 8388608 | tf_op jit(solution)/shard_map/back_transform/pallas_call | solution.py:398
  117.1 5.1 %copy.4 = f32[1792,512]{1,0:T(8,128)} copy(f32[1792,512]{0,1:T(8,128)} %bitcast.4) | data formatting | bytes 7340032 | tf_op jit(solution)/shard_map/transpose | solution.py:416

commit v4 on v3

--- a/solution.py
+++ b/solution.py
@@ -28,12 +28,12 @@
 C_HALF = PANEL // 2
 ORDER = (
     "z0", "z1", "t0", "y0", "z2", "y1", "z3", "y0", "y2", "z4", "y1", "y3", "z5", "y0", "y2",
-    "y4", "z6", "y1", "g1", "c0", "p0", "g1", "p0", "c0", "y3", "y5", "z7", "p0", "g1", "y2",
-    "c0", "p0", "y4", "y6", "y3", "g2", "c1", "g1", "c0", "p1", "g2", "c0", "p0", "s0", "p1",
-    "c1", "p1", "y4", "g2", "y5", "y7", "s0", "g2", "c1", "y6", "g1", "s0", "y5", "c2", "g3",
-    "p1", "c2", "y7", "g2", "c1", "p2", "g3", "p2", "y6", "g1", "p2", "c2", "g3", "y7", "p3",
-    "g2", "p3", "g3", "g1", "c2", "p3", "p2", "c3", "g1", "c1", "p1", "s1", "g3", "c3", "g2",
-    "g2", "g3", "p3", "c2", "p2", "s2", "s1", "c3", "s1", "g3", "c3", "g3", "c3", "p3", "s3",
+    "y4", "z6", "y1", "g1", "c0", "p0", "p0", "c0", "g1", "p0", "y3", "y5", "z7", "y2", "c0",
+    "g1", "p0", "y4", "y6", "y3", "g2", "c1", "p1", "c0", "c1", "p1", "g1", "g2", "p1", "y5",
+    "y7", "c0", "p0", "s0", "y4", "c1", "g2", "p1", "y6", "g1", "s0", "c1", "g2", "y5", "g3",
+    "s0", "g3", "c2", "y7", "p2", "c2", "p2", "g1", "g2", "p2", "g3", "y6", "y7", "c3", "c2",
+    "g2", "p3", "c3", "p3", "g1", "p3", "g3", "p2", "g1", "c1", "p1", "s1", "g2", "g3", "c3",
+    "c2", "g2", "g3", "p3", "c2", "p2", "s2", "s1", "c3", "g3", "s1", "g3", "c3", "p3", "s3",
     "s2", "s2", "s3", "s3",
 )
 
@@ -137,15 +137,20 @@
     def update(b, start):
         at = pl.ds(start, HALF)
         s_high, s_low = split(st[b, at, :])
-
-        @pl.loop(0, ROWS // K)
-        def _(i):
-            lanes = pl.ds(pl.multiple_of(i * K, K), K)
+        for i in range(ROWS // K):
+            lanes = pl.ds(i * K, K)
             fresh = zt[at, lanes] - dot3(s_high, s_low, wh[b, :, lanes], wl[b, :, lanes], NN)
             zt[at, lanes] = fresh
             if b == APPLIED:
                 zh[at, lanes], zl[at, lanes] = split(fresh)
 
+    def store(start, sem):
+        at = pl.ds(start, HALF)
+        copy = pltpu.make_async_copy(zt.at[at], out_ref.at[at], sem)
+        copy.start()
+        stores.append(copy)
+
+    stores = []
     gathered = [None] * len(UNITS)
 
     def z_flow(u):
@@ -320,11 +325,14 @@
         to_core = send(part, part, sc_s.at[b], sc_r.at[b], sibling)
         if b == BLOCKS - 1:
             update(b, mine)
+            store(mine, local_sem.at[0])
         yield
         to_core.wait_recv()
         if b < BLOCKS - 1:
             update(b, mine)
         update(b, theirs)
+        if b == BLOCKS - 1:
+            store(theirs, local_sem.at[1])
         yield
 
     def start(_):
@@ -347,11 +355,10 @@
             steps[name] = flows[name[0]](int(name[1:]))
         next(steps[name])
 
-    store = pltpu.make_async_copy(zt, out_ref, local_sem.at[0])
-    store.start()
     for copy in sent:
         copy.wait_send()
-    store.wait()
+    for copy in stores:
+        copy.wait()
 
 
 def per_device(eigvec, householder, panel_factors):

time: 123 us -> 118 us (0.959)
  Pallas kernels: 117 us -> 112 us
    pallas_call x1, Pallas kernels: 117 us -> 112 us  [per_device(): pl.pallas_call(kernel, out_shape=jax.ShapeDtypeStruct((COLS, ROWS), F32),...]
where the time goes in v4:
time: 118 us; the launch traced here: 117 us
  Pallas kernels  112 us (95%)
  local copies, waits for them, and re-layouts  5.12 us (4%)
    pallas_call x1, Pallas kernels, per_device(): pl.pallas_call(kernel, out_shape=jax.ShapeDtypeStruct((COLS, ROWS), F32),...  112 us
    transpose x1, local copies, waits for them, and re-layouts, per_device(): return turned.T  5.12 us

profile of v4, /device:TPU:1, one launch (start us, length us, event | category | flops | bytes accessed | tf_op | source)
XLA Modules:
  0.0 117.2 jit_solution(11785934022494499392)
XLA Ops:
  0.0 112.1 %back_transform.1 = f32[512,1792]{1,0:T(8,128)} custom-call(f32[1792,512]{1,0:T(8,128)} %z_ref.1, f32[4,2,8,1792]{3,2,1,0:T(8,128)} %bitcast.5, f32[4,2,128,128]{3,2,1,0:T(8,128)} %t_ref.1), custom_call_target="tpu_custom_call" | custom-call | flops 11274289152 | bytes 8388608 | tf_op jit(solution)/shard_map/back_transform/pallas_call | solution.py:405
  112.1 5.1 %copy.4 = f32[1792,512]{1,0:T(8,128)} copy(f32[1792,512]{0,1:T(8,128)} %bitcast.4) | data formatting | bytes 7340032 | tf_op jit(solution)/shard_map/transpose | solution.py:423

commit v5 on v4

--- a/solution.py
+++ b/solution.py
@@ -33,8 +33,8 @@
     "y7", "c0", "p0", "s0", "y4", "c1", "g2", "p1", "y6", "g1", "s0", "c1", "g2", "y5", "g3",
     "s0", "g3", "c2", "y7", "p2", "c2", "p2", "g1", "g2", "p2", "g3", "y6", "y7", "c3", "c2",
     "g2", "p3", "c3", "p3", "g1", "p3", "g3", "p2", "g1", "c1", "p1", "s1", "g2", "g3", "c3",
-    "c2", "g2", "g3", "p3", "c2", "p2", "s2", "s1", "c3", "g3", "s1", "g3", "c3", "p3", "s3",
-    "s2", "s2", "s3", "s3",
+    "c2", "g2", "g3", "p3", "c2", "p2", "s2", "s1", "c3", "g3", "g3", "c3", "p3", "s3", "s2",
+    "s1", "s2", "s3", "s3",
 )
 
 

time: 118 us -> 117 us (level)
  no operation moved by 1% of the time
where the time goes in v5:
time: 117 us
  Pallas kernels  111 us (95%)
  local copies, waits for them, and re-layouts  5.12 us (4%)
    pallas_call x1, Pallas kernels, per_device(): pl.pallas_call(kernel, out_shape=jax.ShapeDtypeStruct((COLS, ROWS), F32),...  111 us
    transpose x1, local copies, waits for them, and re-layouts, per_device(): return turned.T  5.12 us

profile of v5, /device:TPU:1, one launch (start us, length us, event | category | flops | bytes accessed | tf_op | source)
XLA Modules:
  0.0 116.6 jit_solution(7099035760589891766)
XLA Ops:
  0.0 111.4 %back_transform.1 = f32[512,1792]{1,0:T(8,128)} custom-call(f32[1792,512]{1,0:T(8,128)} %z_ref.1, f32[4,2,8,1792]{3,2,1,0:T(8,128)} %bitcast.5, f32[4,2,128,128]{3,2,1,0:T(8,128)} %t_ref.1), custom_call_target="tpu_custom_call" | custom-call | flops 11274289152 | bytes 8388608 | tf_op jit(solution)/shard_map/back_transform/pallas_call | solution.py:405
  111.4 5.1 %copy.4 = f32[1792,512]{1,0:T(8,128)} copy(f32[1792,512]{0,1:T(8,128)} %bitcast.4) | data formatting | bytes 7340032 | tf_op jit(solution)/shard_map/transpose | solution.py:423

commit v6 on v5

--- a/solution.py
+++ b/solution.py
@@ -319,15 +319,18 @@
         to_x = [
             send(part, part, sx_s.at[b, d], sx_r.at[b, d], x_peers[d]) for d in range(3)
         ]
-        yield
-        received(to_x)
-        part = st.at[b, pl.ds(mine, HALF)]
-        to_core = send(part, part, sc_s.at[b], sc_r.at[b], sibling)
+        to_core = [send(part, part, sc_s.at[b, 3], sc_r.at[b, 3], sibling)]
+        yield
+        for d in range(3):
+            to_x[d].wait_recv()
+            at = pl.multiple_of(mine + ((x + 3 - d) % 4) * PIECE, PIECE)
+            part = st.at[b, pl.ds(at, PIECE)]
+            to_core.append(send(part, part, sc_s.at[b, d], sc_r.at[b, d], sibling))
         if b == BLOCKS - 1:
             update(b, mine)
             store(mine, local_sem.at[0])
         yield
-        to_core.wait_recv()
+        received(to_core)
         if b < BLOCKS - 1:
             update(b, mine)
         update(b, theirs)
@@ -399,7 +402,7 @@
         (n,), (n, 3), (n,),
         (n,), (n, 3), (n,), (n,),
         (g,), (g, 3), (g,), (g, 2), (g, 2), (g, 3), (g,),
-        (n, 3), (n,),
+        (n, 3), (n, 4),
     ):
         scratch += [dma(shape), dma(shape)]
     turned = pl.pallas_call(

time: 117 us -> 117 us (level)
  no operation moved by 1% of the time
where the time goes in v6:
time: 117 us
  Pallas kernels  112 us (96%)
  local copies, waits for them, and re-layouts  5.12 us (4%)
    pallas_call x1, Pallas kernels, per_device(): pl.pallas_call(kernel, out_shape=jax.ShapeDtypeStruct((COLS, ROWS), F32),...  112 us
    transpose x1, local copies, waits for them, and re-layouts, per_device(): return turned.T  5.12 us

profile of v6, /device:TPU:1, one launch (start us, length us, event | category | flops | bytes accessed | tf_op | source)
XLA Modules:
  0.0 116.8 jit_solution(6652517047024644302)
XLA Ops:
  0.0 111.7 %back_transform.1 = f32[512,1792]{1,0:T(8,128)} custom-call(f32[1792,512]{1,0:T(8,128)} %z_ref.1, f32[4,2,8,1792]{3,2,1,0:T(8,128)} %bitcast.5, f32[4,2,128,128]{3,2,1,0:T(8,128)} %t_ref.1), custom_call_target="tpu_custom_call" | custom-call | flops 11274289152 | bytes 8388608 | tf_op jit(solution)/shard_map/back_transform/pallas_call | solution.py:408
  111.7 5.1 %copy.4 = f32[1792,512]{1,0:T(8,128)} copy(f32[1792,512]{0,1:T(8,128)} %bitcast.4) | data formatting | bytes 7340032 | tf_op jit(solution)/shard_map/transpose | solution.py:426
